TPU v7x, 32 devices: a whole 2x2x4 slice. The times are simulated.
32 devices in a mesh: dp: 2 (over x), blk: 4 (over y, core), cent: 4 (over z).
Axes of the slice: x: 2, y: 2, z: 4, core: 2. Of those that a mesh axis runs over, the one named last changes fastest.
Arguments:
- embeddings: float32 [16384, 1024], P(('dp', 'blk', 'cent'))
- cluster_ids: int32 [16384, 1], P(('dp', 'blk', 'cent')), may hold values from 0 to 7; in each aligned block of 512 rows (0 to 511, 512 to 1023, ...) at most 96 rows name the same one
- order_index: int32 [16384], P(('dp', 'blk', 'cent')), may hold values from 0 to 16383, each once
- shard_counts: int32 [32], P(('dp', 'blk', 'cent')), may hold values from 1 to 512, 14336 in all
Outputs:
- best_cos: float32 [16384], P(('dp', 'blk', 'cent'))
- centroid: float32 [8, 1024], P(('dp', 'cent'), 'blk')
Inputs may be any that keep to these rules, and one draw needn't show every extreme that they name: `cluster_ids`: among the 512 rows of one shard no cluster id appears more than 96 times, and some id appears exactly 96 times. `order_index`: all values are distinct.
All inputs are finite; a program needn't handle non-finite values. No bound on the sum of `shard_counts` on one device may be relied on, other than what follows from the above.
Results may differ from a plain program's by a relative error of at most 0.0003.
Values may be sent and summed in bfloat16 or wider, within the bound.
A program may use at most 64 MiB of HBM per device.

v0:
```python
import jax
import jax.numpy as jnp
from jax import lax
from jax.sharding import PartitionSpec as P

epsilon = 1e-06
sentinel = 1073741824


def on_device(embeddings, cluster_ids, order_index, shard_counts):
    row_count, features = embeddings.shape
    n_data = lax.axis_size("dp")
    n_owner = lax.axis_size("cent")
    groups = n_data * n_owner
    capacity = 3 * row_count // (2 * groups)
    slot_total = groups * capacity
    member_flag = jnp.arange(row_count, dtype=jnp.int32) < shard_counts[0]
    cluster_col = cluster_ids[:, 0]
    onehot = (
        (cluster_col[:, None] == jnp.arange(groups, dtype=jnp.int32)[None, :])
        & member_flag[:, None]
    ).astype(jnp.int32)
    rank_index = jnp.sum(jnp.cumsum(onehot, axis=0) * onehot, axis=1) - 1
    slot_index = jnp.where(member_flag, cluster_col * capacity + rank_index, slot_total)
    send_rows = (
        jnp.zeros((slot_total, features), jnp.float32).at[slot_index].set(embeddings, mode="drop")
    )
    send_order = (
        jnp.full((slot_total,), sentinel, jnp.int32).at[slot_index].set(order_index, mode="drop")
    )
    got_rows, got_order = (
        lax.all_to_all(
            send_rows.reshape(groups, capacity, features),
            ("dp", "cent"),
            split_axis=0,
            concat_axis=0,
            tiled=True,
        ),
        lax.all_to_all(
            send_order.reshape(groups, capacity),
            ("dp", "cent"),
            split_axis=0,
            concat_axis=0,
            tiled=True,
        ),
    )
    member_rows = got_rows.reshape(slot_total, features)
    member_order = got_order.reshape(slot_total)
    inverse = lax.rsqrt(jnp.mean(member_rows * member_rows, axis=1) + epsilon) / jnp.sqrt(
        jnp.float32(features)
    )
    normed = (member_rows * inverse[:, None]).astype(jnp.bfloat16)
    start_max = jnp.full((slot_total,), -1.0, jnp.float32)
    partner = lax.all_gather(normed, "blk", axis=0, tiled=True)
    partner_order = lax.all_gather(member_order, "blk", axis=0, tiled=True)
    scores = lax.dot_general(
        normed, partner, (((1,), (1,)), ((), ())), preferred_element_type=jnp.float32
    )
    masked = jnp.where(partner_order[None, :] < member_order[:, None], scores, -1.0)
    running = jnp.maximum(start_max, jnp.max(masked, axis=1))
    weight = jnp.where(member_order < sentinel, jax.nn.sigmoid(10.0 * (0.5 - running)), 0.0)
    partial_value = jnp.dot(
        weight[None, :],
        member_rows,
        precision=lax.Precision.HIGHEST,
        preferred_element_type=jnp.float32,
    )
    summed = lax.psum_scatter(partial_value, "blk", scatter_dimension=1, tiled=True)
    weight_sum = lax.psum(jnp.sum(weight), "blk")
    centroid = summed / jnp.sqrt(1.0 + weight_sum)
    home = lax.all_to_all(
        running.reshape(groups, capacity), ("dp", "cent"), split_axis=0, concat_axis=0, tiled=True
    )
    picked = home.reshape(slot_total)[jnp.clip(slot_index, 0, slot_total - 1)]
    best_cos = jnp.where(member_flag, picked, 0.0)
    return (best_cos, centroid)


def solution(mesh):
    placed = (
        P(("dp", "blk", "cent"), None),
        P(("dp", "blk", "cent"), None),
        P(("dp", "blk", "cent")),
        P(("dp", "blk", "cent")),
    )
    return jax.shard_map(
        on_device,
        mesh=mesh,
        in_specs=placed,
        out_specs=(P(("dp", "blk", "cent")), P(("dp", "cent"), "blk")),
        check_vma=False,
    )
```

profile of v0, /device:TPU:0, one launch (start us, length us, event | category | flops | bytes accessed | tf_op | source)
XLA Modules:
  0.0 194.0 jit_solution(2158681941167709992)
XLA Ops:
  7.9 0.7 fusion.5
  8.6 1.1 reduce-window.6
  9.9 0.8 fusion.2
  10.7 0.7 compare_select_fusion
  11.4 5.1 %scatter_custom_fusion.1 = f32[768,1024]{1,0:T(8,128)} fusion(s32[512]{0:T(512)S(1)} %bitcast.50, f32[512,1024]{1,0:T(8,128)} %param.4, f32[]{:T(128)} %constant.8.clone.1), kind=kCustom, calls=%fused_computation.6 | custom fusion | bytes 3146240 | tf_op jit(solution)/shard_map/scatter | solution.py:26
  16.5 78.9 %all_to_all.20 = f32[8,96,1024]{2,1,0:T(8,128)S(1)} all-to-all(f32[8,96,1024]{2,1,0:T(8,128)} %bitcast.40), channel_id=1, replica_groups=mesh['dp'=2,'blk'=4,'cent'=4] {'dp','cent'}, dimensions={0} | all-to-all | bytes 6291456 | tf_op jit(solution)/shard_map/all_to_all | solution.py:32
  95.9 1.4 bitcast_multiply_fusion
  97.3 2.6 %scatter_custom_fusion = s32[768]{0:T(1024)S(1)} fusion(s32[512]{0:T(512)S(1)} %bitcast.51, s32[512]{0:T(512)} %param.6, s32[]{:T(128)} %constant.16.clone.1), kind=kCustom, calls=%fused_computation.26 | custom fusion | bytes 3584 | tf_op jit(solution)/shard_map/scatter | solution.py:29
  99.9 0.7 all_to_all.13
  100.6 3.3 %all-to-all-start = ((s32[8,1,96]{2,1,0:T(1,128)}), s32[8,1,96]{2,1,0:T(1,128)S(1)}, u32[]{:S(2)}, u32[]{:S(2)}) async-start(s32[8,1,96]{2,1,0:T(1,128)} %all_to_all.13), calls=%async_computation | async-start | bytes 8192 | tf_op jit(solution)/shard_map/all_to_all | solution.py:39
  103.9 6.4 %all-to-all-done = s32[8,1,96]{2,1,0:T(1,128)S(1)} async-done(((s32[8,1,96]{2,1,0:T(1,128)}), s32[8,1,96]{2,1,0:T(1,128)S(1)}, u32[]{:S(2)}, u32[]{:S(2)}) %all-to-all-start) | async-done | bytes 3104 | tf_op jit(solution)/shard_map/all_to_all | solution.py:39
  110.8 0.7 reduce.12
  111.6 5.2 %all-gather = s32[4,1,768]{2,1,0:T(1,128)S(1)} all-gather(s32[1,1,768]{2,1,0:T(1,128)S(1)} %reshape.151), channel_id=1, replica_groups=mesh['dp'=2,'blk'=4,'cent'=4] {'blk'}, dimensions={0}, use_global_device_ids=true | all-gather | bytes 15360 | tf_op jit(solution)/shard_map/all_gather | solution.py:55
  116.8 24.4 %all-gather.3.cloned.1.call-done = bf16[3072,1024]{1,0:T(8,128)(2,1)} async-done(((bf16[768,1024]{1,0:T(8,128)(2,1)}), bf16[3072,1024]{1,0:T(8,128)(2,1)}) %all-gather.3.cloned.1.call-update) | async-done | bytes 6291472 | tf_op jit(solution)/shard_map/all_gather | solution.py:54
  141.2 7.8 %select_reduce_fusion = f32[768]{0:T(1024)S(1)} fusion(bf16[768,1024]{1,0:T(8,128)(2,1)} %bitcast_multiply_fusion, bf16[3072,1024]{1,0:T(8,128)(2,1)} %all-gather.3.cloned.1.call-done, s32[3072]{0:T(1024)S(1)} %bitcast.47, s32[768]{0:T(1024)S(1)} %reshape.118), kind=kOutput, calls=%fused_computation.3 | convolution fusion | flops 4838915072 | bytes 7882752 | tf_op jit(solution)/shard_map/dot_general | solution.py:56
  149.1 0.7 max_broadcast_in_dim.20
  149.7 5.5 %all-to-all-start.2 = ((f32[8,1,96]{2,1,0:T(1,128)}), f32[8,1,96]{2,1,0:T(1,128)S(1)}, u32[]{:S(2)}, u32[]{:S(2)}) async-start(f32[8,1,96]{2,1,0:T(1,128)} %max_broadcast_in_dim.20), calls=%async_computation.2 | async-start | bytes 8192 | tf_op jit(solution)/shard_map/all_to_all | solution.py:71
  155.5 0.6 fusion.8
  156.1 7.5 %convolution_bitcast_fusion = f32[1024,1]{1,0:T(8,128)} fusion(f32[8,96,1]{1,2,0:T(1,128)S(1)} %bitcast.46, f32[8,96,1024]{2,1,0:T(8,128)S(1)} %all_to_all.20), kind=kOutput, calls=%fused_computation.8 | convolution fusion | flops 9437184 | bytes 3152896 | tf_op jit(solution)/shard_map/dot_general | solution.py:62
  163.6 6.6 %psum.7 = f32[]{:T(128)} all-reduce(f32[]{:T(128)} %get-tuple-element.2), channel_id=1, replica_groups=mesh['dp'=2,'blk'=4,'cent'=4] {'blk'}, use_global_device_ids=true, to_apply=%region_9.10 | all-reduce | flops 1 | bytes 8 | tf_op jit(solution)/shard_map/psum | solution.py:69
  171.4 0.7 reduce.13
  172.1 2.3 %gather_fusion = f32[512]{0:T(512)S(1)} fusion(f32[768]{0:T(1024)S(1)} %reshape.121, s32[1024]{0:T(1024)S(1)} %pad_clamp_fusion), kind=kCustom, calls=%fused_computation | custom fusion | bytes 6144 | tf_op jit(solution)/shard_map/gather | solution.py:74
  175.0 10.7 %reduce-scatter.4.cloned.1.call-done = f32[256,1]{1,0:T(8,128)} async-done(((f32[1024,1]{1,0:T(8,128)}), f32[256,1]{1,0:T(8,128)}) %reduce-scatter.4.cloned.1.call-update) | async-done | bytes 1040
  185.6 1.0 copy.9
  (25 shorter events, 3.4 us)
Async XLA Ops:
  7.2 134.0 %all-gather.3.cloned.1.call-start = ((), (), s32[]{:S(2)}) async-start(), calls=%async_computation.4 | async-start | bytes 7864320 | tf_op jit(solution)/shard_map/all_gather | solution.py:54
  100.6 9.7 %all-to-all-start = ((s32[8,1,96]{2,1,0:T(1,128)}), s32[8,1,96]{2,1,0:T(1,128)S(1)}, u32[]{:S(2)}, u32[]{:S(2)}) async-start(s32[8,1,96]{2,1,0:T(1,128)} %all_to_all.13), calls=%async_computation | async-start | bytes 8192 | tf_op jit(solution)/shard_map/all_to_all | solution.py:39
  149.7 21.1 %all-to-all-start.2 = ((f32[8,1,96]{2,1,0:T(1,128)}), f32[8,1,96]{2,1,0:T(1,128)S(1)}, u32[]{:S(2)}, u32[]{:S(2)}) async-start(f32[8,1,96]{2,1,0:T(1,128)} %max_broadcast_in_dim.20), calls=%async_computation.2 | async-start | bytes 8192 | tf_op jit(solution)/shard_map/all_to_all | solution.py:71
  155.3 30.4 %reduce-scatter.4.cloned.1.call-start = ((), (), s32[]{:S(2)}) async-start(), calls=%async_computation.5 | async-start | bytes 655360
Sparse Core Ops, SparseCore 0:
  97.4 43.7 all-gather.2
  163.7 21.8 reduce-scatter.3
where the time goes:
time: 195 us; the launch traced here: 194 us
  blocking collectives  90.7 us (47%)
  waiting for transfers between devices  41.4 us (21%)
  between operations  15.5 us (8%)
  matrix products  15.3 us (8%)
  local copies, waits for them, and re-layouts  13.9 us (7%)
  starting transfers between devices  9.08 us (5%)
  other arithmetic  8.13 us (4%)
    all_to_all x1, blocking collectives, on_device(): lax.all_to_all(send_rows.reshape(groups, capacity, features), ('dp', 'cen...  78.9 us
    all_gather x1, waiting for transfers between devices, on_device(): partner = lax.all_gather(normed, 'blk', axis=0, tiled=True)  24.4 us
    unnamed x3, waiting for transfers between devices  10.7 us
    dot_general x1, matrix products, on_device(): lax.dot_general(normed, partner, (((1,), (1,)), ((), ())), preferred_elem...  7.82 us
    dot_general x1, matrix products, on_device(): jnp.dot(weight[None, :], member_rows, precision=lax.Precision.HIGHEST, pr...  7.46 us
    psum x1, blocking collectives, on_device(): weight_sum = lax.psum(jnp.sum(weight), 'blk')  6.56 us
    all_to_all x1, waiting for transfers between devices, on_device(): lax.all_to_all(send_order.reshape(groups, capacity), ('dp', 'cent'), spli...  6.38 us
    all_to_all x1, starting transfers between devices, on_device(): lax.all_to_all(running.reshape(groups, capacity), ('dp', 'cent'), split_a...  5.51 us
  transfers between devices with their start and end apart: 4, of which 3 were waited for; matrix products, arithmetic and copies ran while one was open for 8% of the time, Pallas kernels for 0%

commit v1 on v0

v1 whole, which is shorter than its diff:
```python
import functools

import jax
import jax.numpy as jnp
from jax import lax
from jax.experimental import pallas as pl
from jax.experimental.pallas import tpu as pltpu
from jax.sharding import PartitionSpec as P

epsilon = 1e-06
sentinel = 1073741824.0
MESH = pl.DeviceIdType.MESH
NT = (((1,), (1,)), ((), ()))


def kernel(
    n_dp, n_blk, n_cent, capacity,
    emb, cid_ref, ord_ref, cnt_ref,
    best_ref, cent_ref,
    normed, emb_hi, emb_lo, pack, got, order_out, order_in, order_col,
    home_out, home_in, part, part_in, row_out, row_in,
    a_send, a_recv, o_send, o_recv, c_send, c_recv, y_send, y_recv, d_send, d_recv,
    p_send, p_recv, h_send, h_recv, r_send, r_recv, s_send, s_recv,
):
    groups = n_dp * n_cent
    rows, features = emb.shape
    slots = groups * capacity
    b = lax.axis_index("blk")
    g = lax.axis_index("dp") * n_cent + lax.axis_index("cent")
    chips = n_blk // 2
    other = b + 1 - 2 * lax.rem(b, 2)
    f32, bf16 = jnp.float32, jnp.bfloat16

    def group(index):
        return {"dp": index // n_cent, "cent": lax.rem(index, n_cent)}

    def peer(k):
        return lax.rem(g + k, groups)

    def source(k):
        return lax.rem(g + groups - k, groups)

    def block(index):
        return pl.ds(pl.multiple_of(index * capacity, capacity), capacity)

    def remote(src, dst, send, recv, device):
        return pltpu.make_async_remote_copy(
            src_ref=src, dst_ref=dst, send_sem=send, recv_sem=recv,
            device_id=device, device_id_type=MESH,
        )

    def rows_copy(k):
        return remote(pack.at[block(peer(k))], got.at[b, block(g)], a_send.at[k], a_recv.at[k], group(peer(k)))

    def order_copy(k):
        return remote(order_out.at[peer(k)], order_in.at[b, g], o_send.at[k], o_recv.at[k], group(peer(k)))

    def core_copy(k):
        part_of = got.at[b, block(source(k))]
        return remote(part_of, part_of, c_send.at[k], c_recv.at[k], {"blk": other})

    def chip_copy(m, k):
        part_of = got.at[b, block(source(k))]
        return remote(part_of, part_of, y_send.at[m, k], y_recv.at[m, k], {"blk": lax.rem(b + 2 * m, n_blk)})

    def diagonal_copy(m, k):
        part_of = got.at[lax.rem(b + n_blk - 2 * m, n_blk), block(source(k))]
        return remote(part_of, part_of, d_send.at[m, k], d_recv.at[m, k], {"blk": other})

    def orders_copy(j):
        return remote(order_in.at[b], order_in.at[b], p_send.at[j], p_recv.at[j], {"blk": lax.rem(b + j, n_blk)})

    def home_copy(k):
        return remote(home_out.at[peer(k)], home_in.at[g], h_send.at[k], h_recv.at[k], group(peer(k)))

    def part_copy(j):
        return remote(
            part.at[lax.rem(b + j, n_blk)], part_in.at[b], r_send.at[j], r_recv.at[j], {"blk": lax.rem(b + j, n_blk)}
        )

    def row_copy(k):
        return remote(row_out.at[peer(k)], row_in.at[g], s_send.at[k], s_recv.at[k], group(peer(k)))

    barrier = pltpu.get_barrier_semaphore()
    for k in range(1, groups):
        pl.semaphore_signal(barrier, inc=1, device_id=group(peer(k)), device_id_type=MESH)
    for j in range(1, n_blk):
        pl.semaphore_signal(barrier, inc=1, device_id={"blk": lax.rem(b + j, n_blk)}, device_id_type=MESH)

    step_rows = 64

    @pl.loop(0, rows // step_rows)
    def _(t):
        at = pl.ds(pl.multiple_of(t * step_rows, step_rows), step_rows)
        x = emb[at, :]
        mean = jnp.sum(x * x, axis=1, keepdims=True) * (1.0 / features)
        inverse = lax.rsqrt(mean + epsilon) / jnp.sqrt(f32(features))
        normed[at, :] = (x * inverse).astype(bf16)

    member = lax.broadcasted_iota(jnp.int32, (1, rows), 1) < cnt_ref[...]
    cid = jnp.where(member, cid_ref[...], -1)
    onehot = lax.broadcasted_iota(jnp.int32, (groups, rows), 0) == cid
    onehot_f = jnp.where(onehot, 1.0, 0.0).astype(f32)
    below = lax.broadcasted_iota(jnp.int32, (rows, rows), 0) <= lax.broadcasted_iota(jnp.int32, (rows, rows), 1)
    upto = jnp.dot(
        onehot_f.astype(bf16), jnp.where(below, 1.0, 0.0).astype(bf16), preferred_element_type=f32
    )
    rank = jnp.sum(onehot_f * upto, axis=0, keepdims=True).astype(jnp.int32) - 1
    places = lax.broadcasted_iota(jnp.int32, (128, rows), 0)
    order = ord_ref[...]
    which = lax.broadcasted_iota(jnp.int32, (8, rows), 0)
    pieces = jnp.where(
        which == 0,
        order & 255,
        jnp.where(which == 1, (order >> 8) & 255, jnp.where(which == 2, order >> 16, 1)),
    )
    pieces = pieces.astype(f32).astype(bf16)

    pl.semaphore_wait(barrier, groups + n_blk - 2)

    def packed(c):
        choose = jnp.where(places == jnp.where(cid == c, rank, -1), 1.0, 0.0).astype(bf16)
        data = jnp.dot(choose[:capacity], normed[...], preferred_element_type=f32).astype(bf16)
        found = lax.dot_general(pieces, choose, NT, preferred_element_type=f32)
        value = (
            found[0:1] + 256.0 * found[1:2] + 65536.0 * found[2:3] + (1.0 - found[3:4]) * sentinel
        )
        return data, jnp.broadcast_to(value, (8, 128))

    @pl.loop(1, groups)
    def _(k):
        c = peer(k)
        data, value = packed(c)
        pack[block(c), :] = data
        order_out[c] = value
        rows_copy(k).start()
        order_copy(k).start()

    data, value = packed(g)
    got[b, block(g), :] = data
    order_in[b, g] = value

    def forward(k):
        core_copy(k).start()
        for m in range(1, chips):
            chip_copy(m, k).start()

    def relay(k):
        for m in range(1, chips):
            chip_copy(m, k).wait_recv()
            diagonal_copy(m, k).start()

    forward(0)

    @pl.loop(0, rows // step_rows)
    def _(t):
        at = pl.ds(pl.multiple_of(t * step_rows, step_rows), step_rows)
        x = emb[at, :]
        high = x.astype(bf16)
        emb_hi[at, :] = high
        emb_lo[at, :] = (x - high.astype(f32)).astype(bf16)

    for k in range(1, groups):
        order_copy(k).wait_recv()
    for j in range(1, n_blk):
        orders_copy(j).start()

    @pl.loop(1, groups)
    def _(k):
        rows_copy(k).wait_recv()
        forward(k)
        relay(k - 1)

    relay(groups - 1)

    def columns(j):
        for c in range(groups):
            flat = order_in[j, c].T
            order_col[j, c * capacity:(c + 1) * capacity, :] = jnp.broadcast_to(
                flat[:capacity, 0:1], (capacity, 128)
            )

    columns(b)
    order_row = order_col[b].T[0:1]
    half = slots // 2

    def scores(j, running):
        def one(t, running):
            at = pl.ds(pl.multiple_of(t * half, half), half)
            value = lax.dot_general(got[j, at, :], got[b], NT, preferred_element_type=f32)
            value = jnp.where(order_col[j, at, :][:, 0:1] < order_row, value, -1.0)
            return jnp.maximum(running, jnp.max(value.reshape(half // 8, 8, slots), axis=0))

        return lax.fori_loop(0, 2, one, running)

    running = scores(b, jnp.full((8, slots), -1.0, f32))
    for j in range(1, n_blk):
        orders_copy(j).wait_recv()
    for k in range(groups):
        core_copy(k).wait_recv()
    columns(other)
    running = scores(other, running)
    for m in range(1, chips):
        near = lax.rem(b + n_blk - 2 * m, n_blk)
        columns(near)
        running = scores(near, running)
        for k in range(groups):
            diagonal_copy(m, k).wait_recv()
        far = lax.rem(other + n_blk - 2 * m, n_blk)
        columns(far)
        running = scores(far, running)

    best = jnp.broadcast_to(jnp.max(running, axis=0, keepdims=True), (8, slots))
    for c in range(groups):
        shift = (slots - c * capacity) % slots
        home_out[c] = (pltpu.roll(best, shift, 1) if shift else best)[:, :128]
    for k in range(1, groups):
        home_copy(k).start()
    home_in[g] = home_out[g]
    for k in range(1, groups):
        home_copy(k).wait_recv()

    home = home_in[:, 0, :]
    h1 = home.astype(bf16).astype(f32)
    h2 = (home - h1).astype(bf16).astype(f32)
    h3 = home - h1 - h2
    spread = jnp.where(places == rank, 1.0, 0.0).astype(bf16)
    stack = jnp.concatenate([h1, h2, h3, jnp.zeros_like(h1)], axis=0).astype(bf16)
    table = jnp.dot(stack, spread, preferred_element_type=f32)
    table = table[:groups] + table[groups:2 * groups] + table[2 * groups:3 * groups]
    best_row = jnp.sum(onehot_f * table, axis=0, keepdims=True)
    best_ref[...] = best_row
    keep = onehot_f * (1.0 / (1.0 + jnp.exp(-10.0 * (0.5 - best_row))))
    k1 = keep.astype(bf16).astype(f32)
    both = jnp.concatenate([k1, keep - k1], axis=0).astype(bf16)
    sums = jnp.dot(both, emb_hi[...], preferred_element_type=f32) + jnp.dot(
        both, emb_lo[...], preferred_element_type=f32
    )
    sums = sums[:groups] + sums[groups:]
    weight = jnp.sum(keep, axis=1, keepdims=True)
    width = features // n_blk
    for j in range(n_blk):
        part[j, :, :width] = sums[:, j * width:(j + 1) * width]
        part[j, :, width:] = jnp.broadcast_to(weight, (groups, 128))
    for j in range(1, n_blk):
        part_copy(j).start()
    part_in[b] = part[b]
    for j in range(1, n_blk):
        part_copy(j).wait_recv()
    total = part_in[0]
    for j in range(1, n_blk):
        total = total + part_in[j]
    for c in range(groups):
        row_out[c] = jnp.broadcast_to(total[c:c + 1], (8, width + 128))
    for k in range(1, groups):
        row_copy(k).start()
    row_in[g] = row_out[g]
    for k in range(1, groups):
        row_copy(k).wait_recv()
    final = jnp.sum(row_in[...], axis=0)
    cent_ref[...] = final[0:1, :width] / jnp.sqrt(1.0 + final[0:1, width:width + 1])

    for k in range(groups):
        core_copy(k).wait_send()
        for m in range(1, chips):
            chip_copy(m, k).wait_send()
            diagonal_copy(m, k).wait_send()
    for k in range(1, groups):
        rows_copy(k).wait_send()
        order_copy(k).wait_send()
        home_copy(k).wait_send()
        row_copy(k).wait_send()
    for j in range(1, n_blk):
        orders_copy(j).wait_send()
        part_copy(j).wait_send()


def solution(mesh):
    n_dp, n_blk, n_cent = (mesh.shape[name] for name in ("dp", "blk", "cent"))
    groups = n_dp * n_cent

    def on_device(embeddings, cluster_ids, order_index, shard_counts):
        rows, features = embeddings.shape
        capacity = 3 * rows // (2 * groups)
        capacity = (capacity + 15) // 16 * 16
        slots = groups * capacity
        width = features // n_blk
        f32, bf16 = jnp.float32, jnp.bfloat16
        sem = pltpu.SemaphoreType.DMA
        chips = n_blk // 2
        best, centroid = pl.pallas_call(
            functools.partial(kernel, n_dp, n_blk, n_cent, capacity),
            out_shape=(
                jax.ShapeDtypeStruct((1, rows), f32),
                jax.ShapeDtypeStruct((1, width), f32),
            ),
            in_specs=[pl.BlockSpec(memory_space=pltpu.VMEM)] * 4,
            out_specs=(pl.BlockSpec(memory_space=pltpu.VMEM),) * 2,
            scratch_shapes=[
                pltpu.VMEM((rows, features), bf16),
                pltpu.VMEM((rows, features), bf16),
                pltpu.VMEM((rows, features), bf16),
                pltpu.VMEM((slots, features), bf16),
                pltpu.VMEM((n_blk, slots, features), bf16),
                pltpu.VMEM((groups, 8, 128), f32),
                pltpu.VMEM((n_blk, groups, 8, 128), f32),
                pltpu.VMEM((n_blk, slots, 128), f32),
                pltpu.VMEM((groups, 8, 128), f32),
                pltpu.VMEM((groups, 8, 128), f32),
                pltpu.VMEM((n_blk, groups, width + 128), f32),
                pltpu.VMEM((n_blk, groups, width + 128), f32),
                pltpu.VMEM((groups, 8, width + 128), f32),
                pltpu.VMEM((groups, 8, width + 128), f32),
                sem((groups,)), sem((groups,)), sem((groups,)), sem((groups,)),
                sem((groups,)), sem((groups,)),
                sem((chips, groups)), sem((chips, groups)),
                sem((chips, groups)), sem((chips, groups)),
                sem((n_blk,)), sem((n_blk,)),
                sem((groups,)), sem((groups,)),
                sem((n_blk,)), sem((n_blk,)),
                sem((groups,)), sem((groups,)),
            ],
            compiler_params=pltpu.CompilerParams(
                collective_id=0, has_side_effects=True, vmem_limit_bytes=48 * 1024 * 1024
            ),
        )(
            embeddings,
            cluster_ids.reshape(1, rows),
            order_index.reshape(1, rows),
            shard_counts.reshape(1, 1),
        )
        return best.reshape(rows), centroid

    placed = (
        P(("dp", "blk", "cent"), None),
        P(("dp", "blk", "cent"), None),
        P(("dp", "blk", "cent")),
        P(("dp", "blk", "cent")),
    )
    return jax.shard_map(
        on_device,
        mesh=mesh,
        in_specs=placed,
        out_specs=(P(("dp", "blk", "cent")), P(("dp", "cent"), "blk")),
        check_vma=False,
    )
```

time: 195 us -> 100 us (0.51)
  Pallas kernels: 0 us -> 94.8 us
  blocking collectives: 90.7 us -> 0 us
  waiting for transfers between devices: 41.4 us -> 0 us
  matrix products: 15.3 us -> 0 us
  between operations: 15.5 us -> 1.3 us
  local copies, waits for them, and re-layouts: 13.9 us -> 4.09 us
  starting transfers between devices: 9.08 us -> 0 us
  other arithmetic: 8.13 us -> 0 us
    pallas_call x0 -> x1, Pallas kernels: none -> 94.8 us  [on_device(): pl.pallas_call(functools.partial(kernel, n_dp, n_blk, n_cent, capacity),...]
    all_to_all x1 -> x0, blocking collectives: 78.9 us -> none  [on_device(): lax.all_to_all(send_rows.reshape(groups, capacity, features), ('dp', 'cen...]
    all_gather x1 -> x0, waiting for transfers between devices: 24.4 us -> none  [on_device(): partner = lax.all_gather(normed, 'blk', axis=0, tiled=True)]
    dot_general x2 -> x0, matrix products: 15.3 us -> none  [the longest x1 7.82 us: on_device(): lax.dot_general(normed, partner, (((1,), (1,)), ((), ())), preferred_elem...]
    unnamed x3 -> x0, waiting for transfers between devices: 10.7 us -> none
    all_to_all x2 -> x0, starting transfers between devices: 8.82 us -> none  [the longest x1 5.51 us: on_device(): lax.all_to_all(running.reshape(groups, capacity), ('dp', 'cent'), split_a...]
    scatter x2 -> x0, local copies, waits for them, and re-layouts: 7.71 us -> none  [the longest x1 5.1 us: on_device(): jnp.zeros((slot_total, features), jnp.float32).at[slot_index]]
    psum x1 -> x0, blocking collectives: 6.56 us -> none  [on_device(): weight_sum = lax.psum(jnp.sum(weight), 'blk')]
  transfers between devices with their start and end apart: 4 -> 0, of which waited for: 3 -> 0; matrix products, arithmetic and copies ran while one was open for 8% -> 0% of each run, Pallas kernels for 0% -> 0%
where the time goes in v1:
time: 100 us
  Pallas kernels  94.8 us (95%)
  local copies, waits for them, and re-layouts  4.09 us (4%)
  between operations  1.3 us (1%)
    pallas_call x1, Pallas kernels, on_device(): pl.pallas_call(functools.partial(kernel, n_dp, n_blk, n_cent, capacity),...  94.8 us
    unnamed x8, local copies, waits for them, and re-layouts  4.09 us

profile of v1, /device:TPU:0, one launch (start us, length us, event | category | flops | bytes accessed | tf_op | source)
XLA Modules:
  0.0 100.2 jit_solution(6512969261004844953)
XLA Ops:
  1.3 0.0 copy-start
  1.3 1.6 %copy-done = f32[512,1024]{1,0:T(8,128)S(1)} copy-done((f32[512,1024]{1,0:T(8,128)S(1)}, f32[512,1024]{1,0:T(8,128)}, u32[]{:S(2)}) %copy-start) | copy-done | bytes 2097176
  2.9 0.0 copy-start.1
  2.9 0.7 copy-done.1
  3.6 0.0 copy-start.2
  3.6 0.7 copy-done.2
  4.2 94.8 %shard_map.59 = (f32[1,512]{1,0:T(1,128)S(1)}, f32[1,256]{1,0:T(1,128)S(1)}) custom-call(f32[512,1024]{1,0:T(8,128)S(1)} %copy-done, s32[1,512]{1,0:T(1,128)S(1)} %bitcast.5, s32[1,512]{1,0:T(1,128)S(1)} %bitcast.6, s32[1,1]{1,0:T(1,128)} %bitcast.4.cnt_ref), custom_call_target="tpu_custom_call" | custom-call | tf_op jit(solution)/shard_map/pallas_call | solution.py:291
  99.0 0.6 copy.9
  99.6 0.6 copy.10
Async XLA Ops:
  1.3 1.6 %copy-start = (f32[512,1024]{1,0:T(8,128)S(1)}, f32[512,1024]{1,0:T(8,128)}, u32[]{:S(2)}) copy-start(f32[512,1024]{1,0:T(8,128)} %emb.1) | copy-start | bytes 6291460
  2.9 0.7 copy-start.1
  3.6 0.7 copy-start.2

commit v2 on v1

--- a/solution.py
+++ b/solution.py
@@ -28,6 +28,8 @@
     b = lax.axis_index("blk")
     g = lax.axis_index("dp") * n_cent + lax.axis_index("cent")
     chips = n_blk // 2
+    pieces_per = 2 if capacity % 32 == 0 else 1
+    size = capacity // pieces_per
     other = b + 1 - 2 * lax.rem(b, 2)
     f32, bf16 = jnp.float32, jnp.bfloat16
 
@@ -35,13 +37,18 @@
         return {"dp": index // n_cent, "cent": lax.rem(index, n_cent)}
 
     def peer(k):
-        return lax.rem(g + k, groups)
-
-    def source(k):
-        return lax.rem(g + groups - k, groups)
+        result, bit = g, 1
+        while bit < groups:
+            if (k // bit) % 2:
+                result = result + bit - 2 * bit * lax.rem(g // bit, 2)
+            bit *= 2
+        return result
 
     def block(index):
         return pl.ds(pl.multiple_of(index * capacity, capacity), capacity)
+
+    def piece(index, h):
+        return pl.ds(pl.multiple_of(index * capacity + h * size, size), size)
 
     def remote(src, dst, send, recv, device):
         return pltpu.make_async_remote_copy(
@@ -49,23 +56,27 @@
             device_id=device, device_id_type=MESH,
         )
 
-    def rows_copy(k):
-        return remote(pack.at[block(peer(k))], got.at[b, block(g)], a_send.at[k], a_recv.at[k], group(peer(k)))
+    def rows_copy(k, h):
+        return remote(
+            pack.at[piece(peer(k), h)], got.at[b, piece(g, h)], a_send.at[k, h], a_recv.at[k, h], group(peer(k))
+        )
 
     def order_copy(k):
         return remote(order_out.at[peer(k)], order_in.at[b, g], o_send.at[k], o_recv.at[k], group(peer(k)))
 
-    def core_copy(k):
-        part_of = got.at[b, block(source(k))]
-        return remote(part_of, part_of, c_send.at[k], c_recv.at[k], {"blk": other})
-
-    def chip_copy(m, k):
-        part_of = got.at[b, block(source(k))]
-        return remote(part_of, part_of, y_send.at[m, k], y_recv.at[m, k], {"blk": lax.rem(b + 2 * m, n_blk)})
-
-    def diagonal_copy(m, k):
-        part_of = got.at[lax.rem(b + n_blk - 2 * m, n_blk), block(source(k))]
-        return remote(part_of, part_of, d_send.at[m, k], d_recv.at[m, k], {"blk": other})
+    def core_copy(k, h):
+        part_of = got.at[b, piece(peer(k), h)]
+        return remote(part_of, part_of, c_send.at[k, h], c_recv.at[k, h], {"blk": other})
+
+    def chip_copy(m, k, h):
+        part_of = got.at[b, piece(peer(k), h)]
+        return remote(
+            part_of, part_of, y_send.at[m, k, h], y_recv.at[m, k, h], {"blk": lax.rem(b + 2 * m, n_blk)}
+        )
+
+    def diagonal_copy(m, k, h):
+        part_of = got.at[lax.rem(b + n_blk - 2 * m, n_blk), piece(peer(k), h)]
+        return remote(part_of, part_of, d_send.at[m, k, h], d_recv.at[m, k, h], {"blk": other})
 
     def orders_copy(j):
         return remote(order_in.at[b], order_in.at[b], p_send.at[j], p_recv.at[j], {"blk": lax.rem(b + j, n_blk)})
@@ -127,30 +138,66 @@
         )
         return data, jnp.broadcast_to(value, (8, 128))
 
-    @pl.loop(1, groups)
-    def _(k):
+    span = max(n_cent // 2, 1)
+    far_ones = [k for k in range(1, groups) if (k % n_cent) >= span]
+    near_ones = [k for k in range(1, groups) if (k % n_cent) < span]
+    near_ones.sort(key=lambda k: (k % n_cent) + (k // n_cent) * (k % n_cent > 0) * n_cent)
+    far_units = [(k, h) for k in far_ones for h in range(pieces_per)]
+    near_units = [(k, h) for k in near_ones for h in range(pieces_per)]
+    arrival = [(2 * i + 2.5, u) for i, u in enumerate(far_units)]
+    arrival += [(i + 1, u) for i, u in enumerate(near_units)]
+    arrival = [u for _, u in sorted(arrival)]
+    window = 3
+    waiting = far_units[window:]
+
+    def forward(k, h):
+        core_copy(k, h).start()
+        for m in range(1, chips):
+            chip_copy(m, k, h).start()
+
+    def relay(k, h):
+        for m in range(1, chips):
+            chip_copy(m, k, h).wait_recv()
+            diagonal_copy(m, k, h).start()
+
+    def prepare(k):
         c = peer(k)
         data, value = packed(c)
         pack[block(c), :] = data
         order_out[c] = value
-        rows_copy(k).start()
         order_copy(k).start()
-
+        for h in range(pieces_per):
+            if (k, h) not in waiting:
+                rows_copy(k, h).start()
+
+    prepare(far_ones[0])
+    for k in near_ones[:1]:
+        prepare(k)
     data, value = packed(g)
     got[b, block(g), :] = data
     order_in[b, g] = value
-
-    def forward(k):
-        core_copy(k).start()
-        for m in range(1, chips):
-            chip_copy(m, k).start()
-
-    def relay(k):
-        for m in range(1, chips):
-            chip_copy(m, k).wait_recv()
-            diagonal_copy(m, k).start()
-
-    forward(0)
+    for h in range(pieces_per):
+        forward(0, h)
+    for k in near_ones[1:] + far_ones[1:]:
+        prepare(k)
+
+    done = [(0, h) for h in range(pieces_per)]
+    lag = 2
+    relayed = 0
+    for at_unit in arrival:
+        rows_copy(*at_unit).wait_recv()
+        if at_unit in far_units and waiting:
+            rows_copy(*waiting.pop(0)).start()
+        forward(*at_unit)
+        done.append(at_unit)
+        while relayed < len(done) - lag:
+            relay(*done[relayed])
+            relayed += 1
+
+    for k in range(1, groups):
+        order_copy(k).wait_recv()
+    for j in range(1, n_blk):
+        orders_copy(j).start()
 
     @pl.loop(0, rows // step_rows)
     def _(t):
@@ -160,19 +207,6 @@
         emb_hi[at, :] = high
         emb_lo[at, :] = (x - high.astype(f32)).astype(bf16)
 
-    for k in range(1, groups):
-        order_copy(k).wait_recv()
-    for j in range(1, n_blk):
-        orders_copy(j).start()
-
-    @pl.loop(1, groups)
-    def _(k):
-        rows_copy(k).wait_recv()
-        forward(k)
-        relay(k - 1)
-
-    relay(groups - 1)
-
     def columns(j):
         for c in range(groups):
             flat = order_in[j, c].T
@@ -194,18 +228,20 @@
         return lax.fori_loop(0, 2, one, running)
 
     running = scores(b, jnp.full((8, slots), -1.0, f32))
+    for unit in done[relayed:]:
+        relay(*unit)
     for j in range(1, n_blk):
         orders_copy(j).wait_recv()
-    for k in range(groups):
-        core_copy(k).wait_recv()
+    for unit in done:
+        core_copy(*unit).wait_recv()
     columns(other)
     running = scores(other, running)
     for m in range(1, chips):
         near = lax.rem(b + n_blk - 2 * m, n_blk)
         columns(near)
         running = scores(near, running)
-        for k in range(groups):
-            diagonal_copy(m, k).wait_recv()
+        for unit in done:
+            diagonal_copy(m, *unit).wait_recv()
         far = lax.rem(other + n_blk - 2 * m, n_blk)
         columns(far)
         running = scores(far, running)
@@ -260,13 +296,14 @@
     final = jnp.sum(row_in[...], axis=0)
     cent_ref[...] = final[0:1, :width] / jnp.sqrt(1.0 + final[0:1, width:width + 1])
 
-    for k in range(groups):
-        core_copy(k).wait_send()
+    for unit in done:
+        core_copy(*unit).wait_send()
         for m in range(1, chips):
-            chip_copy(m, k).wait_send()
-            diagonal_copy(m, k).wait_send()
-    for k in range(1, groups):
-        rows_copy(k).wait_send()
+            chip_copy(m, *unit).wait_send()
+            diagonal_copy(m, *unit).wait_send()
+    for unit in arrival:
+        rows_copy(*unit).wait_send()
+    for k in range(1, groups):
         order_copy(k).wait_send()
         home_copy(k).wait_send()
         row_copy(k).wait_send()
@@ -311,10 +348,10 @@
                 pltpu.VMEM((n_blk, groups, width + 128), f32),
                 pltpu.VMEM((groups, 8, width + 128), f32),
                 pltpu.VMEM((groups, 8, width + 128), f32),
-                sem((groups,)), sem((groups,)), sem((groups,)), sem((groups,)),
-                sem((groups,)), sem((groups,)),
-                sem((chips, groups)), sem((chips, groups)),
-                sem((chips, groups)), sem((chips, groups)),
+                sem((groups, 2)), sem((groups, 2)), sem((groups,)), sem((groups,)),
+                sem((groups, 2)), sem((groups, 2)),
+                sem((chips, groups, 2)), sem((chips, groups, 2)),
+                sem((chips, groups, 2)), sem((chips, groups, 2)),
                 sem((n_blk,)), sem((n_blk,)),
                 sem((groups,)), sem((groups,)),
                 sem((n_blk,)), sem((n_blk,)),

time: 100 us -> 72.8 us (0.73)
  Pallas kernels: 94.8 us -> 67.2 us
    pallas_call x1, Pallas kernels: 94.8 us -> 67.2 us  [on_device(): pl.pallas_call(functools.partial(kernel, n_dp, n_blk, n_cent, capacity),...]
where the time goes in v2:
time: 72.8 us; the launch traced here: 72.6 us
  Pallas kernels  67.2 us (92%)
  local copies, waits for them, and re-layouts  4.09 us (6%)
  between operations  1.3 us (2%)
    pallas_call x1, Pallas kernels, on_device(): pl.pallas_call(functools.partial(kernel, n_dp, n_blk, n_cent, capacity),...  67.2 us
    unnamed x8, local copies, waits for them, and re-layouts  4.09 us

profile of v2, /device:TPU:0, one launch (start us, length us, event | category | flops | bytes accessed | tf_op | source)
XLA Modules:
  0.0 72.6 jit_solution(5549048583886811398)
XLA Ops:
  1.3 0.0 copy-start
  1.3 1.6 %copy-done = f32[512,1024]{1,0:T(8,128)S(1)} copy-done((f32[512,1024]{1,0:T(8,128)S(1)}, f32[512,1024]{1,0:T(8,128)}, u32[]{:S(2)}) %copy-start) | copy-done | bytes 2097176
  2.9 0.0 copy-start.1
  2.9 0.7 copy-done.1
  3.6 0.0 copy-start.2
  3.6 0.7 copy-done.2
  4.2 67.2 %shard_map.59 = (f32[1,512]{1,0:T(1,128)S(1)}, f32[1,256]{1,0:T(1,128)S(1)}) custom-call(f32[512,1024]{1,0:T(8,128)S(1)} %copy-done, s32[1,512]{1,0:T(1,128)S(1)} %bitcast.5, s32[1,512]{1,0:T(1,128)S(1)} %bitcast.6, s32[1,1]{1,0:T(1,128)} %bitcast.4.cnt_ref), custom_call_target="tpu_custom_call" | custom-call | tf_op jit(solution)/shard_map/pallas_call | solution.py:328
  71.5 0.6 copy.9
  72.1 0.6 copy.10
Async XLA Ops:
  1.3 1.6 %copy-start = (f32[512,1024]{1,0:T(8,128)S(1)}, f32[512,1024]{1,0:T(8,128)}, u32[]{:S(2)}) copy-start(f32[512,1024]{1,0:T(8,128)} %emb.1) | copy-start | bytes 6291460
  2.9 0.7 copy-start.1
  3.6 0.7 copy-start.2

commit v3 on v2

--- a/solution.py
+++ b/solution.py
@@ -15,15 +15,15 @@
 
 def kernel(
     n_dp, n_blk, n_cent, capacity,
-    emb, cid_ref, ord_ref, cnt_ref,
+    emb_any, cid_any, ord_any, cnt_ref,
     best_ref, cent_ref,
-    normed, emb_hi, emb_lo, pack, got, order_out, order_in, order_col,
+    emb, cid_ref, ord_ref, in_sem, normed, emb_hi, emb_lo, pack, got, order_out, order_in, order_col,
     home_out, home_in, part, part_in, row_out, row_in,
     a_send, a_recv, o_send, o_recv, c_send, c_recv, y_send, y_recv, d_send, d_recv,
     p_send, p_recv, h_send, h_recv, r_send, r_recv, s_send, s_recv,
 ):
     groups = n_dp * n_cent
-    rows, features = emb.shape
+    rows, features = emb_any.shape
     slots = groups * capacity
     b = lax.axis_index("blk")
     g = lax.axis_index("dp") * n_cent + lax.axis_index("cent")
@@ -56,33 +56,47 @@
             device_id=device, device_id_type=MESH,
         )
 
+    span = max(n_cent // 2, 1)
+    far_ones = [k for k in range(1, groups) if (k % n_cent) >= span]
+    near_ones = [k for k in range(1, groups) if (k % n_cent) < span]
+    near_ones.sort(key=lambda k: (k % n_cent) + (k // n_cent) * (k % n_cent > 0) * n_cent)
+    far_units = [(k, h) for k in far_ones for h in range(pieces_per)]
+    near_units = [(k, h) for k in near_ones for h in range(pieces_per)]
+    arrival = [(2 * i + 2.5, u) for i, u in enumerate(far_units)]
+    arrival += [(i + 1, u) for i, u in enumerate(near_units)]
+    arrival = [u for _, u in sorted(arrival)]
+    position = {0: 0}
+    for k, h in arrival:
+        if h == pieces_per - 1:
+            position[k] = len(position)
+
     def rows_copy(k, h):
         return remote(
-            pack.at[piece(peer(k), h)], got.at[b, piece(g, h)], a_send.at[k, h], a_recv.at[k, h], group(peer(k))
+            pack.at[piece(peer(k), h)], got.at[b, piece(position[k], h)], a_send.at[k, h], a_recv.at[k, h], group(peer(k))
         )
 
     def order_copy(k):
-        return remote(order_out.at[peer(k)], order_in.at[b, g], o_send.at[k], o_recv.at[k], group(peer(k)))
+        return remote(order_out.at[peer(k)], order_in.at[b, position[k]], o_send.at[k], o_recv.at[k], group(peer(k)))
 
     def core_copy(k, h):
-        part_of = got.at[b, piece(peer(k), h)]
+        part_of = got.at[b, piece(position[k], h)]
         return remote(part_of, part_of, c_send.at[k, h], c_recv.at[k, h], {"blk": other})
 
     def chip_copy(m, k, h):
-        part_of = got.at[b, piece(peer(k), h)]
+        part_of = got.at[b, piece(position[k], h)]
         return remote(
             part_of, part_of, y_send.at[m, k, h], y_recv.at[m, k, h], {"blk": lax.rem(b + 2 * m, n_blk)}
         )
 
     def diagonal_copy(m, k, h):
-        part_of = got.at[lax.rem(b + n_blk - 2 * m, n_blk), piece(peer(k), h)]
+        part_of = got.at[lax.rem(b + n_blk - 2 * m, n_blk), piece(position[k], h)]
         return remote(part_of, part_of, d_send.at[m, k, h], d_recv.at[m, k, h], {"blk": other})
 
     def orders_copy(j):
         return remote(order_in.at[b], order_in.at[b], p_send.at[j], p_recv.at[j], {"blk": lax.rem(b + j, n_blk)})
 
     def home_copy(k):
-        return remote(home_out.at[peer(k)], home_in.at[g], h_send.at[k], h_recv.at[k], group(peer(k)))
+        return remote(home_out.at[position[k]], home_in.at[g], h_send.at[k], h_recv.at[k], group(peer(k)))
 
     def part_copy(j):
         return remote(
@@ -92,22 +106,30 @@
     def row_copy(k):
         return remote(row_out.at[peer(k)], row_in.at[g], s_send.at[k], s_recv.at[k], group(peer(k)))
 
+    step_rows = 64
+    steps = rows // step_rows
+
+    def chunk(t):
+        return pl.ds(pl.multiple_of(t * step_rows, step_rows), step_rows)
+
+    def load(t):
+        return pltpu.make_async_copy(emb_any.at[chunk(t)], emb.at[chunk(t)], in_sem.at[t])
+
+    load_cid = pltpu.make_async_copy(cid_any, cid_ref, in_sem.at[steps])
+    load_ord = pltpu.make_async_copy(ord_any, ord_ref, in_sem.at[steps + 1])
+    load_cid.start()
+    load_ord.start()
+    for t in range(steps):
+        load(t).start()
+
     barrier = pltpu.get_barrier_semaphore()
     for k in range(1, groups):
         pl.semaphore_signal(barrier, inc=1, device_id=group(peer(k)), device_id_type=MESH)
     for j in range(1, n_blk):
         pl.semaphore_signal(barrier, inc=1, device_id={"blk": lax.rem(b + j, n_blk)}, device_id_type=MESH)
 
-    step_rows = 64
-
-    @pl.loop(0, rows // step_rows)
-    def _(t):
-        at = pl.ds(pl.multiple_of(t * step_rows, step_rows), step_rows)
-        x = emb[at, :]
-        mean = jnp.sum(x * x, axis=1, keepdims=True) * (1.0 / features)
-        inverse = lax.rsqrt(mean + epsilon) / jnp.sqrt(f32(features))
-        normed[at, :] = (x * inverse).astype(bf16)
-
+    load_cid.wait()
+    load_ord.wait()
     member = lax.broadcasted_iota(jnp.int32, (1, rows), 1) < cnt_ref[...]
     cid = jnp.where(member, cid_ref[...], -1)
     onehot = lax.broadcasted_iota(jnp.int32, (groups, rows), 0) == cid
@@ -127,6 +149,15 @@
     )
     pieces = pieces.astype(f32).astype(bf16)
 
+    @pl.loop(0, steps)
+    def _(t):
+        load(t).wait()
+        at = chunk(t)
+        x = emb[at, :]
+        mean = jnp.sum(x * x, axis=1, keepdims=True) * (1.0 / features)
+        inverse = lax.rsqrt(mean + epsilon) / jnp.sqrt(f32(features))
+        normed[at, :] = (x * inverse).astype(bf16)
+
     pl.semaphore_wait(barrier, groups + n_blk - 2)
 
     def packed(c):
@@ -138,15 +169,6 @@
         )
         return data, jnp.broadcast_to(value, (8, 128))
 
-    span = max(n_cent // 2, 1)
-    far_ones = [k for k in range(1, groups) if (k % n_cent) >= span]
-    near_ones = [k for k in range(1, groups) if (k % n_cent) < span]
-    near_ones.sort(key=lambda k: (k % n_cent) + (k // n_cent) * (k % n_cent > 0) * n_cent)
-    far_units = [(k, h) for k in far_ones for h in range(pieces_per)]
-    near_units = [(k, h) for k in near_ones for h in range(pieces_per)]
-    arrival = [(2 * i + 2.5, u) for i, u in enumerate(far_units)]
-    arrival += [(i + 1, u) for i, u in enumerate(near_units)]
-    arrival = [u for _, u in sorted(arrival)]
     window = 3
     waiting = far_units[window:]
 
@@ -174,17 +196,42 @@
     for k in near_ones[:1]:
         prepare(k)
     data, value = packed(g)
-    got[b, block(g), :] = data
-    order_in[b, g] = value
+    got[b, :capacity, :] = data
+    order_in[b, 0] = value
     for h in range(pieces_per):
         forward(0, h)
     for k in near_ones[1:] + far_ones[1:]:
         prepare(k)
 
+    @pl.loop(0, steps)
+    def _(t):
+        at = chunk(t)
+        x = emb[at, :]
+        high = x.astype(bf16)
+        emb_hi[at, :] = high
+        emb_lo[at, :] = (x - high.astype(f32)).astype(bf16)
+
+    def columns(j):
+        for c in range(groups):
+            flat = order_in[j, c].T
+            order_col[j, c * capacity:(c + 1) * capacity, :] = jnp.broadcast_to(
+                flat[:capacity, 0:1], (capacity, 128)
+            )
+
     done = [(0, h) for h in range(pieces_per)]
-    lag = 2
+    lag = 3
     relayed = 0
-    for at_unit in arrival:
+    for number, at_unit in enumerate(arrival):
+        if number == len(arrival) // 2:
+            for k in range(1, groups):
+                order_copy(k).wait_recv()
+            for j in range(1, n_blk):
+                orders_copy(j).start()
+            columns(b)
+        if number == len(arrival) - 2:
+            for j in range(1, n_blk):
+                orders_copy(j).wait_recv()
+                columns(lax.rem(b + n_blk - j, n_blk))
         rows_copy(*at_unit).wait_recv()
         if at_unit in far_units and waiting:
             rows_copy(*waiting.pop(0)).start()
@@ -194,57 +241,40 @@
             relay(*done[relayed])
             relayed += 1
 
-    for k in range(1, groups):
-        order_copy(k).wait_recv()
-    for j in range(1, n_blk):
-        orders_copy(j).start()
-
-    @pl.loop(0, rows // step_rows)
-    def _(t):
-        at = pl.ds(pl.multiple_of(t * step_rows, step_rows), step_rows)
-        x = emb[at, :]
-        high = x.astype(bf16)
-        emb_hi[at, :] = high
-        emb_lo[at, :] = (x - high.astype(f32)).astype(bf16)
-
-    def columns(j):
-        for c in range(groups):
-            flat = order_in[j, c].T
-            order_col[j, c * capacity:(c + 1) * capacity, :] = jnp.broadcast_to(
-                flat[:capacity, 0:1], (capacity, 128)
-            )
-
-    columns(b)
     order_row = order_col[b].T[0:1]
     half = slots // 2
 
-    def scores(j, running):
-        def one(t, running):
-            at = pl.ds(pl.multiple_of(t * half, half), half)
-            value = lax.dot_general(got[j, at, :], got[b], NT, preferred_element_type=f32)
-            value = jnp.where(order_col[j, at, :][:, 0:1] < order_row, value, -1.0)
-            return jnp.maximum(running, jnp.max(value.reshape(half // 8, 8, slots), axis=0))
-
-        return lax.fori_loop(0, 2, one, running)
-
-    running = scores(b, jnp.full((8, slots), -1.0, f32))
-    for unit in done[relayed:]:
-        relay(*unit)
-    for j in range(1, n_blk):
-        orders_copy(j).wait_recv()
+    def scores(j, t, running):
+        at = pl.ds(t * half if isinstance(t, int) else pl.multiple_of(t * half, half), half)
+        value = lax.dot_general(got[j, at, :], got[b], NT, preferred_element_type=f32)
+        value = jnp.where(order_col[j, at, :][:, 0:1] < order_row, value, -1.0)
+        return jnp.maximum(running, jnp.max(value.reshape(half // 8, 8, slots), axis=0))
+
+    def both(j, running):
+        return lax.fori_loop(0, 2, lambda t, r: scores(j, t, r), running)
+
+    first = [u for u in done if position[u[0]] < groups // 2]
+    second = [u for u in done if position[u[0]] >= groups // 2]
+
+    def relay_upto(count):
+        nonlocal relayed
+        while relayed < min(count, len(done)):
+            relay(*done[relayed])
+            relayed += 1
+
+    running = both(b, jnp.full((8, slots), -1.0, f32))
+    relay_upto(len(done) - 2)
     for unit in done:
         core_copy(*unit).wait_recv()
-    columns(other)
-    running = scores(other, running)
-    for m in range(1, chips):
-        near = lax.rem(b + n_blk - 2 * m, n_blk)
-        columns(near)
-        running = scores(near, running)
-        for unit in done:
-            diagonal_copy(m, *unit).wait_recv()
-        far = lax.rem(other + n_blk - 2 * m, n_blk)
-        columns(far)
-        running = scores(far, running)
+    running = both(other, running)
+    for number, (units, t) in enumerate(((first, 0), (second, 1))):
+        if number == 1:
+            relay_upto(len(done))
+        for m in range(1, chips):
+            running = scores(lax.rem(b + n_blk - 2 * m, n_blk), t, running)
+            for unit in units:
+                diagonal_copy(m, *unit).wait_recv()
+            running = scores(lax.rem(other + n_blk - 2 * m, n_blk), t, running)
 
     best = jnp.broadcast_to(jnp.max(running, axis=0, keepdims=True), (8, slots))
     for c in range(groups):
@@ -252,7 +282,7 @@
         home_out[c] = (pltpu.roll(best, shift, 1) if shift else best)[:, :128]
     for k in range(1, groups):
         home_copy(k).start()
-    home_in[g] = home_out[g]
+    home_in[g] = home_out[0]
     for k in range(1, groups):
         home_copy(k).wait_recv()
 
@@ -268,9 +298,9 @@
     best_ref[...] = best_row
     keep = onehot_f * (1.0 / (1.0 + jnp.exp(-10.0 * (0.5 - best_row))))
     k1 = keep.astype(bf16).astype(f32)
-    both = jnp.concatenate([k1, keep - k1], axis=0).astype(bf16)
-    sums = jnp.dot(both, emb_hi[...], preferred_element_type=f32) + jnp.dot(
-        both, emb_lo[...], preferred_element_type=f32
+    pair = jnp.concatenate([k1, keep - k1], axis=0).astype(bf16)
+    sums = jnp.dot(pair, emb_hi[...], preferred_element_type=f32) + jnp.dot(
+        pair, emb_lo[...], preferred_element_type=f32
     )
     sums = sums[:groups] + sums[groups:]
     weight = jnp.sum(keep, axis=1, keepdims=True)
@@ -331,9 +361,13 @@
                 jax.ShapeDtypeStruct((1, rows), f32),
                 jax.ShapeDtypeStruct((1, width), f32),
             ),
-            in_specs=[pl.BlockSpec(memory_space=pltpu.VMEM)] * 4,
+            in_specs=[pl.BlockSpec(memory_space=pl.ANY)] * 3 + [pl.BlockSpec(memory_space=pltpu.VMEM)],
             out_specs=(pl.BlockSpec(memory_space=pltpu.VMEM),) * 2,
             scratch_shapes=[
+                pltpu.VMEM((rows, features), f32),
+                pltpu.VMEM((1, rows), jnp.int32),
+                pltpu.VMEM((1, rows), jnp.int32),
+                sem((rows // 64 + 2,)),
                 pltpu.VMEM((rows, features), bf16),
                 pltpu.VMEM((rows, features), bf16),
                 pltpu.VMEM((rows, features), bf16),

time: 72.8 us -> 69.7 us (0.957)
  Pallas kernels: 67.2 us -> 64.1 us
    pallas_call x1, Pallas kernels: 67.2 us -> 64.1 us  [on_device(): pl.pallas_call(functools.partial(kernel, n_dp, n_blk, n_cent, capacity),...]
where the time goes in v3:
time: 69.7 us; the launch traced here: 69.5 us
  Pallas kernels  64.1 us (92%)
  local copies, waits for them, and re-layouts  4.09 us (6%)
  between operations  1.3 us (2%)
    pallas_call x1, Pallas kernels, on_device(): pl.pallas_call(functools.partial(kernel, n_dp, n_blk, n_cent, capacity),...  64.1 us
    unnamed x8, local copies, waits for them, and re-layouts  4.09 us

profile of v3, /device:TPU:0, one launch (start us, length us, event | category | flops | bytes accessed | tf_op | source)
XLA Modules:
  0.0 69.5 jit_solution(8414848441063128542)
XLA Ops:
  1.3 0.0 copy-start
  1.3 1.6 %copy-done = f32[512,1024]{1,0:T(8,128)S(1)} copy-done((f32[512,1024]{1,0:T(8,128)S(1)}, f32[512,1024]{1,0:T(8,128)}, u32[]{:S(2)}) %copy-start) | copy-done | bytes 2097176
  2.9 0.0 copy-start.1
  2.9 0.7 copy-done.1
  3.6 0.0 copy-start.2
  3.6 0.7 copy-done.2
  4.2 64.1 %shard_map.59 = (f32[1,512]{1,0:T(1,128)S(1)}, f32[1,256]{1,0:T(1,128)S(1)}) custom-call(f32[512,1024]{1,0:T(8,128)S(1)} %copy-done, s32[1,512]{1,0:T(1,128)S(1)} %bitcast.5, s32[1,512]{1,0:T(1,128)S(1)} %bitcast.6, s32[1,1]{1,0:T(1,128)} %bitcast.4.cnt_ref), custom_call_target="tpu_custom_call" | custom-call | tf_op jit(solution)/shard_map/pallas_call | solution.py:358
  68.3 0.6 copy.9
  68.9 0.6 copy.10
Async XLA Ops:
  1.3 1.6 %copy-start = (f32[512,1024]{1,0:T(8,128)S(1)}, f32[512,1024]{1,0:T(8,128)}, u32[]{:S(2)}) copy-start(f32[512,1024]{1,0:T(8,128)} %emb_any.1) | copy-start | bytes 6291460
  2.9 0.7 copy-start.1
  3.6 0.7 copy-start.2
